TPU v7x, 256 devices: a whole 4x4x8 slice. The times are simulated.
256 devices in a mesh: worker: 8 (over y, z_hi), fsdp: 32 (over z_lo, x, core).
Axes of the slice: x: 4, y: 4, z: 8 (z_hi: 2, z_lo: 4; z = z_hi * 4 + z_lo), core: 2. Of those that a mesh axis runs over, the one named last changes fastest.
Arguments:
- activations: bfloat16 [131072, 4608], P(('worker', 'fsdp')), may hold values from -6 to 6
- key_target: bfloat16 [131072, 1024], P(('worker', 'fsdp')), may hold values from -6 to 6
- key_weight: bfloat16 [36864, 1024], P(('worker', 'fsdp')), may hold values from -0.09375 to 0.09375
- fragment_base: float32 [512, 4608], P('fsdp'), may hold values from -6 to 6
- fragment_momentum: float32 [512, 4608], P('fsdp'), may hold values from -6 to 6
- delta_codes: int32 [4096, 4608], P(('worker', 'fsdp')), may hold values from 0 to 15
- block_scale: float32 [4096, 36], P(('worker', 'fsdp')), may hold values from 0.5 to 5
- code_table: float32 [16], replicated, may hold values from -1 to 1
Outputs:
- weight_grad: float32 [36864, 1024], P(('worker', 'fsdp'))
- input_grad: bfloat16 [131072, 4608], P(('worker', 'fsdp'))
- new_base: float32 [512, 4608], P('fsdp')
- new_momentum: float32 [512, 4608], P('fsdp')
All inputs are finite; a program needn't handle non-finite values.
Results may differ from a plain program's by a relative error of at most 0.0047.
Values may be sent and summed in bfloat16 or wider, within the bound.
A program may use at most 128 MiB of HBM per device.

v0:
```python
import jax
import jax.numpy as jnp
from jax import lax
from jax.sharding import PartitionSpec as P

BLOCK = 128


outer_rate = 0.7
outer_momentum = 0.9


def outer_update(mean_delta, base_rows, momentum_rows):
    momentum_next = outer_momentum * momentum_rows + mean_delta
    base_next = base_rows - outer_rate * (mean_delta + outer_momentum * momentum_next)
    return (base_next, momentum_next)


def body(
    activations,
    key_target,
    key_weight,
    fragment_base,
    fragment_momentum,
    delta_codes,
    block_scale,
    code_table,
):
    fsdp_size = lax.axis_size("fsdp")
    group_tokens = activations.shape[0] * fsdp_size
    gathered = lax.all_gather(key_weight, "fsdp", axis=0, tiled=True)
    projected = jnp.dot(activations, gathered, preferred_element_type=jnp.float32)
    errors = (projected - key_target.astype(jnp.float32)).astype(jnp.bfloat16)
    backward = lax.dot_general(
        errors, gathered, (((1,), (1,)), ((), ())), preferred_element_type=jnp.float32
    )
    input_grad = backward.astype(jnp.bfloat16)
    summed = lax.psum_scatter(
        lax.dot_general(
            activations, errors, (((0,), (0,)), ((), ())), preferred_element_type=jnp.float32
        ),
        "fsdp",
        scatter_dimension=0,
        tiled=True,
    )
    weight_grad = summed / jnp.sqrt(jnp.float32(group_tokens))
    levels = jnp.arange(code_table.shape[0], dtype=jnp.int32)
    matches = delta_codes[:, :, None] == levels
    values = jnp.sum(jnp.where(matches, code_table, jnp.float32(0.0)), axis=-1)
    rows_here = delta_codes.shape[0]
    width = delta_codes.shape[1]
    deltas = (values.reshape(rows_here, width // BLOCK, BLOCK) * block_scale[:, :, None]).reshape(
        rows_here, width
    )
    workers = lax.axis_size("worker")
    total_delta = lax.psum(deltas, "worker")
    mean_delta = total_delta / workers
    new_base, new_momentum = outer_update(mean_delta, fragment_base, fragment_momentum)
    return (weight_grad, input_grad, new_base, new_momentum)


def solution(mesh):
    placed = (
        P(("worker", "fsdp"), None),
        P(("worker", "fsdp"), None),
        P(("worker", "fsdp"), None),
        P("fsdp", None),
        P("fsdp", None),
        P(("worker", "fsdp"), None),
        P(("worker", "fsdp"), None),
        P(),
    )
    return jax.shard_map(
        body,
        mesh=mesh,
        in_specs=placed,
        out_specs=(
            P(("worker", "fsdp"), None),
            P(("worker", "fsdp"), None),
            P("fsdp", None),
            P("fsdp", None),
        ),
        check_vma=False,
    )
```

profile of v0, /device:TPU:24, one launch (start us, length us, event | category | flops | bytes accessed | tf_op | source)
XLA Modules:
  0.0 317.1 jit_solution(8773881287580392995)
XLA Ops:
  8.0 0.0 all-gather.2.cloned.1.call-start
  8.0 0.7 all-gather.2.cloned.1.call-update
  8.7 0.0 all-reduce.2.cloned.1.call-start
  8.8 2.1 select_reduce_fusion
  10.9 0.8 mul.23
  11.7 0.8 bitcast_multiply_fusion
  12.5 0.0 all-reduce.2.cloned.1.call-update
  12.5 0.0 copy-start
  12.5 0.0 reduce-scatter.4.cloned.1.call-start
  12.6 79.2 %all-gather.2.cloned.1.call-done = bf16[4608,1024]{1,0:T(8,128)(2,1)} async-done(((bf16[144,1024]{1,0:T(8,128)(2,1)}), bf16[4608,1024]{1,0:T(8,128)(2,1)}) %all-gather.2.cloned.1.call-update) | async-done | bytes 9437200 | tf_op jit(solution)/shard_map/all_gather | solution.py:31
  91.8 9.0 %fusion.2 = f32[512,1024]{1,0:T(8,128)S(1)} fusion(bf16[512,4608]{1,0:T(8,128)(2,1)} %param.8, bf16[4608,1024]{1,0:T(8,128)(2,1)} %all-gather.2.cloned.1.call-done), kind=kOutput, calls=%fused_computation.11 | convolution fusion | flops 4831838208 | bytes 16252928 | tf_op jit(solution)/shard_map/dot_general | solution.py:32
  100.8 0.0 copy-done
  100.8 11.5 %convolution_bitcast_fusion = f32[4608,1024]{0,1:T(8,128)} fusion(bf16[512,4608]{1,0:T(8,128)(2,1)} %param.8, f32[512,1024]{1,0:T(8,128)S(1)} %fusion.2, bf16[512,1024]{1,0:T(8,128)(2,1)S(1)} %copy-done), kind=kOutput, calls=%fused_computation | convolution fusion | flops 4833411072 | bytes 26738688 | tf_op jit(solution)/shard_map/dot_general | solution.py:39
  112.3 18.6 %copy.16 = f32[4608,1024]{1,0:T(8,128)} copy(f32[4608,1024]{0,1:T(8,128)} %convolution_bitcast_fusion) | data formatting | bytes 37748736
  131.0 0.0 copy-start.1
  131.0 0.0 reduce-scatter.4.cloned.1.call-update
  131.0 1.0 all-reduce.2.cloned.1.call-done
  132.0 0.0 copy-done.1
  132.0 1.9 multiply_subtract_fusion
  133.9 10.4 %convolution_convert_fusion = bf16[512,4608]{1,0:T(8,128)(2,1)} fusion(bf16[4608,1024]{1,0:T(8,128)(2,1)} %all-gather.2.cloned.1.call-done, f32[512,1024]{1,0:T(8,128)S(1)} %fusion.2, bf16[512,1024]{1,0:T(8,128)(2,1)S(1)} %copy-done), kind=kOutput, calls=%fused_computation.1 | convolution fusion | flops 4835770368 | bytes 17301504 | tf_op jit(solution)/shard_map/dot_general | solution.py:34
  144.3 162.7 %reduce-scatter.4.cloned.1.call-done = f32[144,1024]{1,0:T(8,128)} async-done(((f32[4608,1024]{1,0:T(8,128)}), f32[144,1024]{1,0:T(8,128)}) %reduce-scatter.4.cloned.1.call-update) | async-done | bytes 589840
  307.1 1.4 copy.17
  308.5 0.1 broadcast_multiply_fusion
  308.5 1.1 copy.15
Async XLA Ops:
  8.0 83.8 %all-gather.2.cloned.1.call-start = ((), (), s32[]{:S(2)}) async-start(), calls=%async_computation.1 | async-start | bytes 9732096 | tf_op jit(solution)/shard_map/all_gather | solution.py:31
  8.7 123.3 %all-reduce.2.cloned.1.call-start = ((), (), s32[]{:S(2)}) async-start(), calls=%async_computation.2 | async-start | bytes 589824 | tf_op jit(solution)/shard_map/psum | solution.py:56
  12.5 88.3 %copy-start = (bf16[512,1024]{1,0:T(8,128)(2,1)S(1)}, bf16[512,1024]{1,0:T(8,128)(2,1)}, u32[]{:S(2)}) copy-start(bf16[512,1024]{1,0:T(8,128)(2,1)} %param.9) | copy-start | bytes 3145732
  12.5 294.5 %reduce-scatter.4.cloned.1.call-start = ((), (), s32[]{:S(2)}) async-start(), calls=%async_computation.3 | async-start | bytes 19464192
  131.0 1.0 copy-start.1
Sparse Core Ops, SparseCore 0:
  10.7 81.0 all-gather.1
  131.1 175.8 reduce-scatter.3
Sparse Core Ops, SparseCore 1:
  12.6 119.3 all-reduce.1
where the time goes:
time: 318 us; the launch traced here: 317 us
  waiting for transfers between devices  244 us (77%)
  matrix products  30.9 us (10%)
  local copies, waits for them, and re-layouts  22 us (7%)
  between operations  15.5 us (5%)
  other arithmetic  4.88 us (2%)
    unnamed x4, waiting for transfers between devices  163 us
    all_gather x1, waiting for transfers between devices, body(): gathered = lax.all_gather(key_weight, 'fsdp', axis=0, tiled=True)  79.2 us
    unnamed x7, local copies, waits for them, and re-layouts  21.2 us
    dot_general x1, matrix products, body(): lax.dot_general(activations, errors, (((0,), (0,)), ((), ())), preferred_...  11.5 us
    dot_general x1, matrix products, body(): lax.dot_general(errors, gathered, (((1,), (1,)), ((), ())), preferred_ele...  10.4 us
    dot_general x1, matrix products, body(): jnp.dot(activations, gathered, preferred_element_type=jnp.float32)  8.99 us
  transfers between devices with their start and end apart: 3, of which 3 were waited for; matrix products, arithmetic and copies ran while one was open for 17% of the time, Pallas kernels for 0%

commit v1 on v0

v1 whole, which is shorter than its diff:
```python
import functools

import jax
import jax.numpy as jnp
from jax import lax
from jax.experimental import pallas as pl
from jax.experimental.pallas import tpu as pltpu
from jax.sharding import PartitionSpec as P

BLOCK = 128
NZ, NX, NC = 4, 4, 2
PARTS = 4

MESH = pl.DeviceIdType.MESH
F32, BF16 = jnp.float32, jnp.bfloat16

outer_rate = 0.7
outer_momentum = 0.9


def outer_update(mean_delta, base_rows, momentum_rows):
    momentum_next = outer_momentum * momentum_rows + mean_delta
    base_next = base_rows - outer_rate * (mean_delta + outer_momentum * momentum_next)
    return (base_next, momentum_next)


def kernel(
    a_hbm, t_hbm, w_hbm, wg_hbm, ig_hbm,
    a, at, t, w, e, g, dr, x2r, x1r, zr, wg, ig,
    lsem, wsem, tsem, osem,
    ag_s, ag_r, rs_s, rs_r,
):
    tokens, d = a.shape
    rows, cw = w.shape[4], w.shape[5]
    scale = 1.0 / (tokens * NZ * NX * NC) ** 0.5
    wk = lax.axis_index("worker")
    f = lax.axis_index("fsdp")
    z, x, c = f // (NX * NC), lax.rem(f // NC, NX), lax.rem(f, NC)
    xp, xm, xo, co = lax.rem(x + 1, NX), lax.rem(x + 3, NX), lax.rem(x + 2, NX), 1 - c

    def dev(zz, xx, cc):
        return (wk, (zz * NX + xx) * NC + cc)

    zup = [lax.rem(z + k, NZ) for k in range(NZ)]
    zdn = [lax.rem(z + NZ - k, NZ) for k in range(NZ)]
    DP, DM, DS = dev(z, xp, c), dev(z, xm, c), dev(z, x, co)

    for s in range(PARTS):
        cols = pl.ds(s * cw, cw)
        pltpu.make_async_copy(w_hbm.at[:, cols], w.at[s, z, x, c], wsem.at[s]).start()
    pltpu.make_async_copy(a_hbm, a, lsem).start()
    for s in range(PARTS):
        pltpu.make_async_copy(t_hbm.at[:, pl.ds(s * cw, cw)], t.at[s], tsem.at[s]).start()

    barrier = pltpu.get_barrier_semaphore()
    partners = [dev(zup[k], x, c) for k in (1, 2, 3)] + [DP, DM, DS]
    for p in partners:
        pl.semaphore_signal(barrier, inc=1, device_id=p, device_id_type=MESH)
    pl.semaphore_wait(barrier, len(partners))

    sent = []

    def send(src, dst, ss, rs, to):
        cp = pltpu.make_async_remote_copy(
            src_ref=src, dst_ref=dst, send_sem=ss, recv_sem=rs, device_id=to, device_id_type=MESH
        )
        cp.start()
        sent.append(cp)

    def arrive(dst, rs):
        pltpu.make_async_remote_copy(
            src_ref=dst, dst_ref=dst, send_sem=rs, recv_sem=rs, device_id=DS, device_id_type=MESH
        ).wait_recv()

    def z_send(s):
        pltpu.make_async_copy(w_hbm.at[:, pl.ds(s * cw, cw)], w.at[s, z, x, c], wsem.at[s]).wait()
        for k in (3, 2, 1):
            blk = w.at[s, z, x, c]
            send(blk, blk, ag_s.at[s, k], ag_r.at[s, k], dev(zup[k], x, c))

    def z_wait(s):
        for k in (1, 2, 3):
            arrive(w.at[s, zdn[k], x, c], ag_r.at[s, k])

    def x1_send(s):
        line = w.at[s, :, x, c]
        send(line, line, ag_s.at[s, 4], ag_r.at[s, 4], DP)
        send(line, line, ag_s.at[s, 5], ag_r.at[s, 5], DM)

    def x2_send(s):
        arrive(w.at[s, :, xm, c], ag_r.at[s, 4])
        up = w.at[s, pl.ds(0, 2), xm, c]
        send(up, up, ag_s.at[s, 6], ag_r.at[s, 6], DP)
        arrive(w.at[s, :, xp, c], ag_r.at[s, 5])
        down = w.at[s, pl.ds(2, 2), xp, c]
        send(down, down, ag_s.at[s, 7], ag_r.at[s, 7], DM)

    def x2_wait(s):
        arrive(w.at[s, pl.ds(0, 2), xo, c], ag_r.at[s, 6])
        arrive(w.at[s, pl.ds(2, 2), xo, c], ag_r.at[s, 7])

    def d_send(s, k):
        line = w.at[s, :, (x, xp, xm, xo)[k], c]
        send(line, line, ag_s.at[s, 8 + k], ag_r.at[s, 8 + k], DS)

    def d_wait(s):
        for k in range(4):
            arrive(w.at[s, :, (x, xp, xm, xo)[k], co], ag_r.at[s, 8 + k])

    def transpose():
        pltpu.make_async_copy(a_hbm, a, lsem).wait()
        slab = d // NZ
        for j in range(NZ):
            at[j] = a[:, j * slab : (j + 1) * slab].T.reshape(NX, NC * rows, tokens)

    mt = min(256, tokens)

    def project(s):
        pltpu.make_async_copy(t_hbm.at[:, pl.ds(s * cw, cw)], t.at[s], tsem.at[s]).wait()

        @pl.loop(0, tokens // mt)
        def _(m):
            r = pl.ds(pl.multiple_of(m * mt, mt), mt)
            p = jnp.dot(a[r, :], w[s].reshape(d, cw), preferred_element_type=F32)
            e[s, r, :] = (p - t[s, r, :].astype(F32)).astype(BF16)

    def grad_rows(s, k):
        xt = (xo, xp, xm, x)[k]

        @pl.loop(0, NZ)
        def _(j):
            q = jnp.dot(at[j, xt], e[s], preferred_element_type=F32)
            g[s, j, xt] = q.astype(BF16).reshape(NC, rows, cw)

        send(g.at[s, :, xt, co], dr.at[s, :, xt], rs_s.at[s, k], rs_r.at[s, k], DS)

    def back(j):
        slab = d // NZ
        c0 = j * slab

        @pl.loop(0, tokens // mt)
        def _(m):
            r = pl.ds(pl.multiple_of(m * mt, mt), mt)
            acc = None
            for s in range(PARTS):
                q = lax.dot_general(
                    e[s, r, :], w[s, j].reshape(slab, cw), (((1,), (1,)), ((), ())),
                    preferred_element_type=F32,
                )
                acc = q if acc is None else acc + q
            ig[r, c0 : c0 + slab] = acc.astype(BF16)

        pltpu.make_async_copy(ig.at[:, pl.ds(c0, slab)], ig_hbm.at[:, pl.ds(c0, slab)], osem.at[j]).start()

    def rx2(s):
        arrive(dr.at[s, :, xo], rs_r.at[s, 0])

        @pl.loop(0, NZ)
        def _(j):
            g[s, j, xo, c] = (g[s, j, xo, c].astype(F32) + dr[s, j, xo].astype(F32)).astype(BF16)

        send(g.at[s, pl.ds(0, 2), xo, c], x2r.at[s, 0], rs_s.at[s, 4], rs_r.at[s, 4], DP)
        send(g.at[s, pl.ds(2, 2), xo, c], x2r.at[s, 1], rs_s.at[s, 5], rs_r.at[s, 5], DM)

    def rx1(s):
        arrive(dr.at[s, :, xp], rs_r.at[s, 1])
        arrive(dr.at[s, :, xm], rs_r.at[s, 2])
        arrive(x2r.at[s, 0], rs_r.at[s, 4])
        arrive(x2r.at[s, 1], rs_r.at[s, 5])
        for j in range(NZ):
            up = g[s, j, xp, c].astype(F32) + dr[s, j, xp].astype(F32)
            if j < 2:
                up = up + x2r[s, 0, j].astype(F32)
            g[s, j, xp, c] = up.astype(BF16)
        send(g.at[s, :, xp, c], x1r.at[s, 0], rs_s.at[s, 6], rs_r.at[s, 6], DP)
        for j in range(NZ):
            down = g[s, j, xm, c].astype(F32) + dr[s, j, xm].astype(F32)
            if j >= 2:
                down = down + x2r[s, 1, j - 2].astype(F32)
            g[s, j, xm, c] = down.astype(BF16)
        send(g.at[s, :, xm, c], x1r.at[s, 1], rs_s.at[s, 7], rs_r.at[s, 7], DM)

    def x_sum(s, j):
        return (
            g[s, j, x, c].astype(F32)
            + dr[s, j, x].astype(F32)
            + x1r[s, 0, j].astype(F32)
            + x1r[s, 1, j].astype(F32)
        )

    def rz(s):
        arrive(dr.at[s, :, x], rs_r.at[s, 3])
        arrive(x1r.at[s, 0], rs_r.at[s, 6])
        arrive(x1r.at[s, 1], rs_r.at[s, 7])
        for k in (3, 2, 1):
            j = zup[k]
            g[s, j, x, c] = x_sum(s, j).astype(BF16)
            send(g.at[s, j, x, c], zr.at[s, k - 1], rs_s.at[s, 7 + k], rs_r.at[s, 7 + k], dev(j, x, c))
        wg[:, s * cw : (s + 1) * cw] = x_sum(s, z)

    def rf(s):
        for k in (1, 2, 3):
            arrive(zr.at[s, k - 1], rs_r.at[s, 7 + k])
        cols = slice(s * cw, (s + 1) * cw)
        total = wg[:, cols]
        for k in range(3):
            total = total + zr[s, k].astype(F32)
        wg[:, cols] = total * scale
        pltpu.make_async_copy(
            wg.at[:, pl.ds(s * cw, cw)], wg_hbm.at[:, pl.ds(s * cw, cw)], osem.at[NZ + s]
        ).start()

    last = PARTS - 1
    z_send(0)
    transpose()
    z_wait(0)
    x1_send(0)
    z_send(1)
    d_send(0, 0)
    for s in range(PARTS):
        x2_send(s)
        d_send(s, 1)
        d_send(s, 2)
        if s < last:
            z_wait(s + 1)
            x1_send(s + 1)
            d_send(s + 1, 0)
        if s + 1 < last:
            z_send(s + 2)
        x2_wait(s)
        d_send(s, 3)
        if s > 0:
            rx1(s - 1)
        d_wait(s)
        project(s)
        for k in range(4):
            grad_rows(s, k)
        if s > 0:
            rz(s - 1)
        rx2(s)
        if s > 0:
            rf(s - 1)
    back(0)
    rx1(last)
    back(1)
    back(2)
    rz(last)
    back(3)
    rf(last)

    for cp in sent:
        cp.wait_send()
    slab = d // NZ
    for j in range(NZ):
        cols = pl.ds(j * slab, slab)
        pltpu.make_async_copy(ig.at[:, cols], ig_hbm.at[:, cols], osem.at[j]).wait()
    for s in range(PARTS):
        cols = pl.ds(s * cw, cw)
        pltpu.make_async_copy(wg.at[:, cols], wg_hbm.at[:, cols], osem.at[NZ + s]).wait()


def inner_step(activations, key_target, key_weight):
    tokens, d = activations.shape
    rows, kv = key_weight.shape
    cw = kv // PARTS
    blk = (rows, cw)
    dma = pltpu.SemaphoreType.DMA
    return pl.pallas_call(
        kernel,
        out_shape=(
            jax.ShapeDtypeStruct((rows, kv), F32),
            jax.ShapeDtypeStruct((tokens, d), BF16),
        ),
        in_specs=[pl.BlockSpec(memory_space=pl.ANY)] * 3,
        out_specs=[pl.BlockSpec(memory_space=pl.ANY)] * 2,
        scratch_shapes=[
            pltpu.VMEM((tokens, d), BF16),
            pltpu.VMEM((NZ, NX, NC * rows, tokens), BF16),
            pltpu.VMEM((PARTS, tokens, cw), BF16),
            pltpu.VMEM((PARTS, NZ, NX, NC) + blk, BF16),
            pltpu.VMEM((PARTS, tokens, cw), BF16),
            pltpu.VMEM((PARTS, NZ, NX, NC) + blk, BF16),
            pltpu.VMEM((PARTS, NZ, NX) + blk, BF16),
            pltpu.VMEM((PARTS, 2, 2) + blk, BF16),
            pltpu.VMEM((PARTS, 2, NZ) + blk, BF16),
            pltpu.VMEM((PARTS, NZ - 1) + blk, BF16),
            pltpu.VMEM((rows, kv), F32),
            pltpu.VMEM((tokens, d), BF16),
            dma,
            dma((PARTS,)),
            dma((PARTS,)),
            dma((NZ + PARTS,)),
            dma((PARTS, 12)),
            dma((PARTS, 12)),
            dma((PARTS, 11)),
            dma((PARTS, 11)),
        ],
        compiler_params=pltpu.CompilerParams(
            collective_id=0, has_side_effects=True, vmem_limit_bytes=60 * 2**20
        ),
        cost_estimate=pl.CostEstimate(
            flops=6 * tokens * d * kv, bytes_accessed=64 * 2**20, transcendentals=0
        ),
        name="inner_step",
    )(activations, key_target, key_weight)


def body(
    activations,
    key_target,
    key_weight,
    fragment_base,
    fragment_momentum,
    delta_codes,
    block_scale,
    code_table,
):
    levels = jnp.arange(code_table.shape[0], dtype=jnp.int32)
    matches = delta_codes[:, :, None] == levels
    values = jnp.sum(jnp.where(matches, code_table, jnp.float32(0.0)), axis=-1)
    rows_here = delta_codes.shape[0]
    width = delta_codes.shape[1]
    deltas = (values.reshape(rows_here, width // BLOCK, BLOCK) * block_scale[:, :, None]).reshape(
        rows_here, width
    )
    workers = lax.axis_size("worker")
    total_delta = lax.psum(deltas, "worker")
    weight_grad, input_grad = inner_step(activations, key_target, key_weight)
    mean_delta = total_delta / workers
    new_base, new_momentum = outer_update(mean_delta, fragment_base, fragment_momentum)
    return (weight_grad, input_grad, new_base, new_momentum)


def solution(mesh):
    placed = (
        P(("worker", "fsdp"), None),
        P(("worker", "fsdp"), None),
        P(("worker", "fsdp"), None),
        P("fsdp", None),
        P("fsdp", None),
        P(("worker", "fsdp"), None),
        P(("worker", "fsdp"), None),
        P(),
    )
    return jax.shard_map(
        body,
        mesh=mesh,
        in_specs=placed,
        out_specs=(
            P(("worker", "fsdp"), None),
            P(("worker", "fsdp"), None),
            P("fsdp", None),
            P("fsdp", None),
        ),
        check_vma=False,
    )
```

time: 318 us -> 160 us (0.50)
  the two profiles are of different devices: /device:TPU:24 before, /device:TPU:10 now
where the time goes in v1:
time: 160 us; the launch traced here: 159 us
  Pallas kernels  133 us (83%)
  between operations  14.1 us (9%)
  local copies, waits for them, and re-layouts  7.6 us (5%)
  other arithmetic  4.72 us (3%)
    pallas_call x1, Pallas kernels, inner_step(): pl.pallas_call(kernel, out_shape=(jax.ShapeDtypeStruct((rows, kv), F32),...  133 us
    unnamed x6, local copies, waits for them, and re-layouts  6.77 us
  transfers between devices with their start and end apart: 1, of which 0 were waited for; matrix products, arithmetic and copies ran while one was open for 0% of the time, Pallas kernels for 83%

profile of v1, /device:TPU:10, one launch (start us, length us, event | category | flops | bytes accessed | tf_op | source)
XLA Modules:
  0.0 159.4 jit_solution(13770877522207830556)
XLA Ops:
  7.2 0.0 all-reduce.2.cloned.1.call-start
  7.2 2.1 %select_reduce_fusion = f32[16,4608]{1,0:T(8,128)S(1)} fusion(f32[16]{0:T(128)} %param.15, s32[16,4608]{1,0:T(8,128)} %param.13), kind=kLoop, calls=%fused_computation | loop fusion | flops 3465216 | bytes 589888 | tf_op jit(solution)/shard_map/reduce_sum | solution.py:320
  9.3 0.8 mul.23
  10.2 0.8 bitcast_multiply_fusion
  10.9 0.0 all-reduce.2.cloned.1.call-update
  11.0 0.0 copy-start
  11.0 0.0 copy-start.1
  11.0 132.9 %inner_step.1 = (f32[144,1024]{1,0:T(8,128)}, bf16[512,4608]{1,0:T(8,128)(2,1)}) custom-call(bf16[512,4608]{1,0:T(8,128)(2,1)} %a_hbm.1, bf16[512,1024]{1,0:T(8,128)(2,1)} %t_hbm.1, bf16[144,1024]{1,0:T(8,128)(2,1)} %w_hbm.1), custom_call_target="tpu_custom_call" | custom-call | flops 14495514624 | bytes 67108864 | tf_op jit(solution)/shard_map/inner_step/pallas_call | solution.py:268
  143.9 0.0 all-reduce.2.cloned.1.call-done
  143.9 0.0 copy-done
  143.9 0.0 copy-done.1
  143.9 1.9 %multiply_subtract_fusion = (f32[16,4608]{1,0:T(8,128)}, f32[16,4608]{1,0:T(8,128)}) fusion(f32[16,4608]{1,0:T(8,128)S(1)} %copy-done, f32[16,4608]{1,0:T(8,128)} %all-reduce.2.cloned.1.call-done, f32[16,4608]{1,0:T(8,128)S(1)} %copy-done.1), kind=kLoop, calls=%fused_computation.3 | loop fusion | flops 516096 | bytes 1474560 | tf_op jit(solution)/shard_map/sub | solution.py:23
  145.8 1.9 %copy.17 = f32[144,1024]{1,0:T(8,128)} copy(f32[144,1024]{1,0:T(8,128)} %get-tuple-element.14) | data formatting | bytes 1179648
  147.7 4.8 %copy.18 = bf16[512,4608]{1,0:T(8,128)(2,1)} copy(bf16[512,4608]{1,0:T(8,128)(2,1)} %get-tuple-element.15) | data formatting | bytes 9437184
Async XLA Ops:
  7.2 136.8 %all-reduce.2.cloned.1.call-start = ((), (), s32[]{:S(2)}) async-start(), calls=%async_computation | async-start | bytes 589824 | tf_op jit(solution)/shard_map/psum | solution.py:327
  11.0 133.0 %copy-start = (f32[16,4608]{1,0:T(8,128)S(1)}, f32[16,4608]{1,0:T(8,128)}, u32[]{:S(2)}) copy-start(f32[16,4608]{1,0:T(8,128)} %param.11) | copy-start | bytes 884740
  11.0 133.0 %copy-start.1 = (f32[16,4608]{1,0:T(8,128)S(1)}, f32[16,4608]{1,0:T(8,128)}, u32[]{:S(2)}) copy-start(f32[16,4608]{1,0:T(8,128)} %param.12) | copy-start | bytes 884740
Sparse Core Ops, SparseCore 0:
  11.2 113.9 all-reduce.1

commit v2 on v0

v2 whole, which is shorter than its diff:
```python
import jax
import jax.numpy as jnp
from jax import lax
from jax.experimental import pallas as pl
from jax.experimental.pallas import tpu as pltpu
from jax.sharding import PartitionSpec as P

BLOCK = 128
NZ, NX, NC = 4, 4, 2
NY, NH = 4, 2
WIDTHS = (1, 2, 2, 2, 1)
MIXED = (0, 1, 1, 1, 0)

MESH = pl.DeviceIdType.MESH
F32, BF16 = jnp.float32, jnp.bfloat16

outer_rate = 0.7
outer_momentum = 0.9


def outer_update(mean_delta, base_rows, momentum_rows):
    momentum_next = outer_momentum * momentum_rows + mean_delta
    base_next = base_rows - outer_rate * (mean_delta + outer_momentum * momentum_next)
    return (base_next, momentum_next)


def kernel(
    table, a_hbm, t_hbm, w_hbm, code_hbm, scale_hbm,
    wg_hbm, ig_hbm, mean_hbm,
    a, at, t, w, e, g, dr, x2r, x1r, zr, zc, hx2, hx1, wg, ig,
    code, bscale, dl, dyr, dz, mean,
    lsem, csem, wsem, tsem, osem, isem, msem,
    ag_s, ag_r, rs_s, rs_r, dl_s, dl_r,
):
    parts = len(w)
    tokens, d = a.shape
    rows = w[0].shape[3]
    width = [p.shape[4] for p in w]
    start = [sum(width[:s]) for s in range(parts)]
    half = rows // 9
    low = [rows - 2 * half * m for m in MIXED]
    lows = [pl.ds(0, n) for n in low]
    first = rows - 2 * half
    hi, hi0, hi1 = pl.ds(first, 2 * half), pl.ds(first, half), pl.ds(first + half, half)
    scale = 1.0 / (tokens * NZ * NX * NC) ** 0.5
    slab = d // NZ
    quarter = d // NY

    wk = lax.axis_index("worker")
    f = lax.axis_index("fsdp")
    y, h = wk // NH, lax.rem(wk, NH)
    z, x, c = f // (NX * NC), lax.rem(f // NC, NX), lax.rem(f, NC)
    xp, xm, xo, co = lax.rem(x + 1, NX), lax.rem(x + 3, NX), lax.rem(x + 2, NX), 1 - c
    lines = (xo, xp, xm, x)

    def dev(zz, xx, cc):
        return (wk, (zz * NX + xx) * NC + cc)

    zup = [lax.rem(z + k, NZ) for k in range(NZ)]
    zdn = [lax.rem(z + NZ - k, NZ) for k in range(NZ)]
    yup = [lax.rem(y + k, NY) for k in range(NY)]
    ydn = [lax.rem(y + NY - k, NY) for k in range(NY)]
    DP, DM, DS = dev(z, xp, c), dev(z, xm, c), dev(z, x, co)
    DU, DD = dev(lax.rem(z + 1, NZ), x, c), dev(lax.rem(z + 3, NZ), x, c)
    DH = (y * NH + 1 - h, f)

    def cols(s):
        return pl.ds(start[s], width[s])

    def w_in(s):
        return pltpu.make_async_copy(w_hbm.at[:, cols(s)], w[s].at[z, x, c], wsem.at[s])

    def t_in(s):
        return pltpu.make_async_copy(t_hbm.at[:, cols(s)], t[s], tsem.at[s])

    a_in = pltpu.make_async_copy(a_hbm, a, lsem)
    code_in = pltpu.make_async_copy(code_hbm, code, csem.at[0])
    scale_in = pltpu.make_async_copy(scale_hbm, bscale, csem.at[1])

    for s in range(parts):
        w_in(s).start()
    code_in.start()
    scale_in.start()
    a_in.start()
    for s in range(parts):
        t_in(s).start()

    barrier = pltpu.get_barrier_semaphore()
    partners = [dev(zup[k], x, c) for k in (1, 2, 3)] + [DP, DM, DS, DH]
    partners += [(yup[k] * NH + h, f) for k in (1, 2, 3)]
    for p in partners:
        pl.semaphore_signal(barrier, inc=1, device_id=p, device_id_type=MESH)
    pl.semaphore_wait(barrier, len(partners))

    sent = []

    def send(src, dst, ss, rs, to, cond=None):
        cp = pltpu.make_async_remote_copy(
            src_ref=src, dst_ref=dst, send_sem=ss, recv_sem=rs, device_id=to, device_id_type=MESH
        )
        if cond is None:
            cp.start()
        else:
            pl.when(cond)(cp.start)
        sent.append((cp, cond))

    def arrive(dst, rs):
        pltpu.make_async_remote_copy(
            src_ref=dst, dst_ref=dst, send_sem=rs, recv_sem=rs, device_id=DS, device_id_type=MESH
        ).wait_recv()

    def guard(ok):
        def wrap(step):
            def run(s, *k):
                if ok(s):
                    step(s, *k)

            return run

        return wrap

    there = guard(lambda s: 0 <= s < parts)
    if_mixed = guard(lambda s: 0 <= s < parts and MIXED[s])

    @there
    def z_send(s):
        w_in(s).wait()
        for k in (3, 2, 1):
            blk = w[s].at[z, x, c, lows[s]]
            send(blk, blk, ag_s.at[s, k - 1], ag_r.at[s, k - 1], dev(zup[k], x, c))

    @there
    def z_wait(s):
        for k in (1, 2, 3):
            arrive(w[s].at[zdn[k], x, c, lows[s]], ag_r.at[s, k - 1])

    @there
    def x1_send(s):
        line = w[s].at[:, x, c, lows[s]]
        send(line, line, ag_s.at[s, 3], ag_r.at[s, 3], DP)
        send(line, line, ag_s.at[s, 4], ag_r.at[s, 4], DM)

    @there
    def x2_send(s):
        arrive(w[s].at[:, xm, c, lows[s]], ag_r.at[s, 3])
        up = w[s].at[pl.ds(0, 2), xm, c, lows[s]]
        send(up, up, ag_s.at[s, 5], ag_r.at[s, 5], DP)
        arrive(w[s].at[:, xp, c, lows[s]], ag_r.at[s, 4])
        down = w[s].at[pl.ds(2, 2), xp, c, lows[s]]
        send(down, down, ag_s.at[s, 6], ag_r.at[s, 6], DM)

    @there
    def x2_wait(s):
        arrive(w[s].at[pl.ds(0, 2), xo, c, lows[s]], ag_r.at[s, 5])
        arrive(w[s].at[pl.ds(2, 2), xo, c, lows[s]], ag_r.at[s, 6])

    @there
    def d_send(s, k):
        line = w[s].at[:, lines[k], c, lows[s]]
        send(line, line, ag_s.at[s, 7 + k], ag_r.at[s, 7 + k], DS)

    @if_mixed
    def d_send_hi(s):
        rest = w[s].at[:, :, c, hi]
        send(rest, rest, ag_s.at[s, 11], ag_r.at[s, 11], DS)

    @there
    def d_wait(s):
        for k in range(4):
            arrive(w[s].at[:, lines[k], co, lows[s]], ag_r.at[s, 7 + k])
        if MIXED[s]:
            arrive(w[s].at[:, :, co, hi], ag_r.at[s, 11])

    @if_mixed
    def h1_send(s):
        blk = w[s].at[z, x, c, hi]
        send(blk, blk, ag_s.at[s, 12], ag_r.at[s, 12], DP)
        send(blk, blk, ag_s.at[s, 13], ag_r.at[s, 13], DM)

    @if_mixed
    def h2_send(s):
        arrive(w[s].at[z, xm, c, hi], ag_r.at[s, 12])
        up = w[s].at[z, xm, c, hi0]
        send(up, up, ag_s.at[s, 14], ag_r.at[s, 14], DP)
        arrive(w[s].at[z, xp, c, hi], ag_r.at[s, 13])
        down = w[s].at[z, xp, c, hi1]
        send(down, down, ag_s.at[s, 15], ag_r.at[s, 15], DM)

    @if_mixed
    def h2_wait(s):
        arrive(w[s].at[z, xo, c, hi0], ag_r.at[s, 14])
        arrive(w[s].at[z, xo, c, hi1], ag_r.at[s, 15])

    @if_mixed
    def hop_send(s, k):
        up, dn = w[s].at[zdn[k - 1], :, c, hi], w[s].at[zup[k - 1], :, c, hi]
        send(up, up, ag_s.at[s, 15 + k], ag_r.at[s, 15 + k], DU, (z >= k - 1) & (z < NZ - 1))
        send(dn, dn, ag_s.at[s, 18 + k], ag_r.at[s, 18 + k], DD, (z + k <= NZ) & (z > 0))

    @if_mixed
    def hop_wait(s, k):
        pl.when(z >= k)(lambda: arrive(w[s].at[zdn[k], :, c, hi], ag_r.at[s, 15 + k]))
        pl.when(z + k < NZ)(lambda: arrive(w[s].at[zup[k], :, c, hi], ag_r.at[s, 18 + k]))

    def transpose():
        a_in.wait()
        for j in range(NZ):
            at[j] = a[:, j * slab : (j + 1) * slab].T.reshape(NX, NC * rows, tokens)

    @there
    def project(s):
        t_in(s).wait()
        p = jnp.dot(a[...], w[s][...].reshape(d, width[s]), preferred_element_type=F32)
        e[s][...] = (p - t[s][...].astype(F32)).astype(BF16)

    @there
    def grad_rows(s, k):
        xt = lines[k]
        q = jnp.dot(at[:, xt].reshape(slab, tokens), e[s][...], preferred_element_type=F32)
        g[s][:, xt] = q.astype(BF16).reshape(NZ, NC, rows, width[s])
        send(g[s].at[:, xt, co], dr[s].at[:, xt], rs_s.at[s, k], rs_r.at[s, k], DS)

    def back(j):
        er = jnp.concatenate([e[s][...] for s in range(parts)], axis=1)
        wr = jnp.concatenate([w[s][j].reshape(slab, width[s]) for s in range(parts)], axis=1)
        q = lax.dot_general(er, wr, (((1,), (1,)), ((), ())), preferred_element_type=F32)
        ig[:, j * slab : (j + 1) * slab] = q.astype(BF16)
        ig_out(j).start()

    def ig_out(j):
        here = pl.ds(j * slab, slab)
        return pltpu.make_async_copy(ig.at[:, here], ig_hbm.at[:, here], isem.at[j])

    def wg_out(s):
        return pltpu.make_async_copy(wg.at[:, cols(s)], wg_hbm.at[:, cols(s)], osem.at[s])

    def plus(u, v):
        return u.astype(F32) + v.astype(F32)

    def merge(s, k):
        xt = lines[k]
        arrive(dr[s].at[:, xt], rs_r.at[s, k])
        g[s][:, xt, c] = plus(g[s][:, xt, c], dr[s][:, xt]).astype(BF16)

    @there
    def r1(s):
        merge(s, 0)
        send(g[s].at[pl.ds(0, 2), xo, c, lows[s]], x2r[s].at[0], rs_s.at[s, 4], rs_r.at[s, 4], DP)
        send(g[s].at[pl.ds(2, 2), xo, c, lows[s]], x2r[s].at[1], rs_s.at[s, 5], rs_r.at[s, 5], DM)
        for k in (1, 2, 3):
            merge(s, k)
        if MIXED[s]:
            hop(s, 1)

    def hop(s, k):
        up, dn = zup[NZ - k], zdn[NZ - k]
        goes_up, goes_dn = z <= k - 1, z >= NZ - k
        if k > 1:

            @pl.when(goes_up & (z > 0))
            def _():
                arrive(zc[s].at[0, k - 2], rs_r.at[s, 9 + k])
                g[s][up, :, c, first:] = plus(g[s][up, :, c, first:], zc[s][0, k - 2]).astype(BF16)

            @pl.when(goes_dn & (z < NZ - 1))
            def _():
                arrive(zc[s].at[1, k - 2], rs_r.at[s, 12 + k])
                g[s][dn, :, c, first:] = plus(g[s][dn, :, c, first:], zc[s][1, k - 2]).astype(BF16)

        send(g[s].at[up, :, c, hi], zc[s].at[0, k - 1], rs_s.at[s, 10 + k], rs_r.at[s, 10 + k], DU, goes_up)
        send(g[s].at[dn, :, c, hi], zc[s].at[1, k - 1], rs_s.at[s, 13 + k], rs_r.at[s, 13 + k], DD, goes_dn)

    @there
    def r2(s):
        arrive(x2r[s].at[0], rs_r.at[s, 4])
        g[s][0:2, xp, c, :low[s]] = plus(g[s][0:2, xp, c, :low[s]], x2r[s][0]).astype(BF16)
        send(g[s].at[:, xp, c, lows[s]], x1r[s].at[0], rs_s.at[s, 6], rs_r.at[s, 6], DP)
        arrive(x2r[s].at[1], rs_r.at[s, 5])
        g[s][2:4, xm, c, :low[s]] = plus(g[s][2:4, xm, c, :low[s]], x2r[s][1]).astype(BF16)
        send(g[s].at[:, xm, c, lows[s]], x1r[s].at[1], rs_s.at[s, 7], rs_r.at[s, 7], DM)
        if MIXED[s]:
            hop(s, 2)

    @there
    def r3(s):
        arrive(x1r[s].at[0], rs_r.at[s, 6])
        arrive(x1r[s].at[1], rs_r.at[s, 7])

        def x_sum(j):
            return plus(g[s][j, x, c, :low[s]], x1r[s][0, j]) + x1r[s][1, j].astype(F32)

        for k in (3, 2, 1):
            j = zup[k]
            g[s][j, x, c, :low[s]] = x_sum(j).astype(BF16)
            send(g[s].at[j, x, c, lows[s]], zr[s].at[k - 1], rs_s.at[s, 7 + k], rs_r.at[s, 7 + k], dev(j, x, c))
        wg[: low[s], start[s] : start[s] + width[s]] = x_sum(z)
        if MIXED[s]:
            hop(s, 3)

    @if_mixed
    def r4(s):
        @pl.when(z > 0)
        def _():
            arrive(zc[s].at[0, 2], rs_r.at[s, 13])
            g[s][z, :, c, first:] = plus(g[s][z, :, c, first:], zc[s][0, 2]).astype(BF16)

        @pl.when(z < NZ - 1)
        def _():
            arrive(zc[s].at[1, 2], rs_r.at[s, 16])
            g[s][z, :, c, first:] = plus(g[s][z, :, c, first:], zc[s][1, 2]).astype(BF16)

        send(g[s].at[z, xo, c, hi0], hx2[s].at[0], rs_s.at[s, 17], rs_r.at[s, 17], DP)
        send(g[s].at[z, xo, c, hi1], hx2[s].at[1], rs_s.at[s, 18], rs_r.at[s, 18], DM)

    @if_mixed
    def r5(s):
        arrive(hx2[s].at[0], rs_r.at[s, 17])
        g[s][z, xp, c, first : first + half] = plus(g[s][z, xp, c, first : first + half], hx2[s][0]).astype(BF16)
        send(g[s].at[z, xp, c, hi], hx1[s].at[0], rs_s.at[s, 19], rs_r.at[s, 19], DP)
        arrive(hx2[s].at[1], rs_r.at[s, 18])
        g[s][z, xm, c, first + half :] = plus(g[s][z, xm, c, first + half :], hx2[s][1]).astype(BF16)
        send(g[s].at[z, xm, c, hi], hx1[s].at[1], rs_s.at[s, 20], rs_r.at[s, 20], DM)

    @there
    def r6(s):
        here = slice(start[s], start[s] + width[s])
        total = wg[: low[s], here]
        for k in (1, 2, 3):
            arrive(zr[s].at[k - 1], rs_r.at[s, 7 + k])
            total = total + zr[s][k - 1].astype(F32)
        wg[: low[s], here] = total * scale
        if MIXED[s]:
            arrive(hx1[s].at[0], rs_r.at[s, 19])
            arrive(hx1[s].at[1], rs_r.at[s, 20])
            rest = plus(g[s][z, x, c, first:], hx1[s][0]) + hx1[s][1].astype(F32)
            wg[first:, here] = rest * scale
        wg_out(s).start()

    def delta_send():
        code_in.wait()
        scale_in.wait()
        for q in range(NY):
            for b in range(quarter // BLOCK):
                at_col = q * quarter + b * BLOCK
                levels = code[:, at_col : at_col + BLOCK]
                v = jnp.full(levels.shape, table[0], F32)
                for i in range(1, table.shape[0]):
                    v = jnp.where(levels == i, table[i], v)
                n = at_col // BLOCK
                dl[q, :, b * BLOCK : (b + 1) * BLOCK] = v * bscale[:, n : n + 1]
        for k in (1, 2, 3):
            send(dl.at[yup[k]], dyr.at[k - 1], dl_s.at[k - 1], dl_r.at[k - 1], (yup[k] * NH + h, f))

    def delta_pair():
        total = dl[y]
        for k in (1, 2, 3):
            arrive(dyr.at[k - 1], dl_r.at[k - 1])
            total = total + dyr[k - 1]
        dz[0] = total.astype(BF16)
        send(dz.at[0], dz.at[1], dl_s.at[3], dl_r.at[3], DH)

    def delta_share():
        arrive(dz.at[1], dl_r.at[3])
        mean[y] = plus(dz[0], dz[1]) / (NY * NH)
        for k in (1, 2, 3):
            send(mean.at[y], mean.at[y], dl_s.at[3 + k], dl_r.at[3 + k], (yup[k] * NH + h, f))

    def mean_out(q):
        return pltpu.make_async_copy(mean.at[q], mean_hbm.at[:, pl.ds(q * quarter, quarter)], msem.at[q])

    def delta_out():
        for k in (1, 2, 3):
            arrive(mean.at[ydn[k]], dl_r.at[3 + k])
        for q in range(NY):
            mean_out(q).start()

    z_send(0)
    z_send(1)
    h1_send(1)
    delta_send()
    z_wait(0)
    x1_send(0)
    d_send(0, 3)
    h2_send(1)
    z_send(2)
    h1_send(2)
    transpose()
    delta_pair()
    z_wait(1)
    x1_send(1)
    d_send(1, 3)
    for i in range(parts + 1):
        h2_wait(i + 1)
        hop_send(i + 1, 1)
        hop_wait(i, 2)
        hop_send(i, 3)
        x2_send(i)
        d_send(i, 1)
        d_send(i, 2)
        z_send(i + 3)
        h1_send(i + 3)
        h2_send(i + 2)
        z_wait(i + 2)
        x1_send(i + 2)
        d_send(i + 2, 3)
        r1(i - 2)
        r2(i - 3)
        r3(i - 4)
        d_wait(i - 1)
        project(i - 1)
        x2_wait(i)
        d_send(i, 0)
        hop_wait(i + 1, 1)
        hop_send(i + 1, 2)
        for k in range(4):
            grad_rows(i - 1, k)
        hop_wait(i, 3)
        d_send_hi(i)
        if i == 1:
            delta_share()
        if i == 2:
            delta_out()
    for i in range(parts + 1, parts + 5):
        r1(i - 2)
        r2(i - 3)
        r3(i - 4)
        r4(i - 5)
        r5(i - 6)
        r6(i - 6)
        back(i - parts - 1)
    r6(parts - 1)

    for cp, cond in sent:
        if cond is None:
            cp.wait_send()
        else:
            pl.when(cond)(cp.wait_send)
    for j in range(NZ):
        ig_out(j).wait()
    for s in range(parts):
        wg_out(s).wait()
    for q in range(NY):
        mean_out(q).wait()


def inner_step(activations, key_target, key_weight, delta_codes, block_scale, code_table):
    tokens, d = activations.shape
    rows, kv = key_weight.shape
    frag = delta_codes.shape[0]
    widths = [kv * n // sum(WIDTHS) for n in WIDTHS]
    parts = len(widths)
    half = rows // 9
    nhi = 2 * half
    low = [rows - nhi * m for m in MIXED]
    dma = pltpu.SemaphoreType.DMA

    def each(*shape):
        return [pltpu.VMEM(shape + (cw,), BF16) for cw in widths]

    anywhere = pl.BlockSpec(memory_space=pl.ANY)
    return pl.pallas_call(
        kernel,
        out_shape=(
            jax.ShapeDtypeStruct((rows, kv), F32),
            jax.ShapeDtypeStruct((tokens, d), BF16),
            jax.ShapeDtypeStruct((frag, d), F32),
        ),
        in_specs=[pl.BlockSpec(memory_space=pltpu.SMEM)] + [anywhere] * 5,
        out_specs=[anywhere] * 3,
        scratch_shapes=[
            pltpu.VMEM((tokens, d), BF16),
            pltpu.VMEM((NZ, NX, NC * rows, tokens), BF16),
            each(tokens),
            each(NZ, NX, NC, rows),
            each(tokens),
            each(NZ, NX, NC, rows),
            each(NZ, NX, rows),
            [pltpu.VMEM((2, 2, n, cw), BF16) for n, cw in zip(low, widths)],
            [pltpu.VMEM((2, NZ, n, cw), BF16) for n, cw in zip(low, widths)],
            [pltpu.VMEM((NZ - 1, n, cw), BF16) for n, cw in zip(low, widths)],
            each(2, NZ - 1, NX, nhi),
            each(2, half),
            each(2, nhi),
            pltpu.VMEM((rows, kv), F32),
            pltpu.VMEM((tokens, d), BF16),
            pltpu.VMEM(delta_codes.shape, jnp.int32),
            pltpu.VMEM(block_scale.shape, F32),
            pltpu.VMEM((NY, frag, d // NY), F32),
            pltpu.VMEM((NY - 1, frag, d // NY), F32),
            pltpu.VMEM((NH, frag, d // NY), BF16),
            pltpu.VMEM((NY, frag, d // NY), F32),
            dma,
            dma((2,)),
            dma((parts,)),
            dma((parts,)),
            dma((parts,)),
            dma((NZ,)),
            dma((NY,)),
            dma((parts, 22)),
            dma((parts, 22)),
            dma((parts, 21)),
            dma((parts, 21)),
            dma((7,)),
            dma((7,)),
        ],
        compiler_params=pltpu.CompilerParams(
            collective_id=0, has_side_effects=True, vmem_limit_bytes=60 * 2**20
        ),
        cost_estimate=pl.CostEstimate(
            flops=6 * tokens * d * kv, bytes_accessed=64 * 2**20, transcendentals=0
        ),
        name="inner_step",
    )(code_table, activations, key_target, key_weight, delta_codes, block_scale)


def finish_kernel(
    wg_in, ig_in, mean_in, base_in, mom_in, wg_out, ig_out, base_out, mom_out,
    wg, ig, mean, base, mom, base_next, mom_next, sem_in, sem_out,
):
    n = sem_in.shape[0] - 4
    rows = ig.shape[0] // n

    def piece(ref, i):
        return ref.at[pl.ds(i * rows, rows)]

    small = [(mean_in, mean), (base_in, base), (mom_in, mom), (wg_in, wg)]
    get = [pltpu.make_async_copy(u, v, sem_in.at[n + i]) for i, (u, v) in enumerate(small)]
    fetch = [pltpu.make_async_copy(piece(ig_in, i), piece(ig, i), sem_in.at[i]) for i in range(n)]
    done = [pltpu.make_async_copy(piece(ig, i), piece(ig_out, i), sem_out.at[i]) for i in range(n)]
    small = [(base_next, base_out), (mom_next, mom_out), (wg, wg_out)]
    put = [pltpu.make_async_copy(u, v, sem_out.at[n + i]) for i, (u, v) in enumerate(small)]
    for cp in fetch[:2] + get + fetch[2:]:
        cp.start()
    for i in range(2):
        fetch[i].wait()
        done[i].start()
    for cp in get[:3]:
        cp.wait()
    base_next[...], mom_next[...] = outer_update(mean[...], base[...], mom[...])
    put[0].start()
    put[1].start()
    get[3].wait()
    put[2].start()
    for i in range(2, n):
        fetch[i].wait()
        done[i].start()
    for cp in done + put:
        cp.wait()


def finish(weight_grad, input_grad, mean_delta, base, momentum):
    pieces = 8
    anywhere = pl.BlockSpec(memory_space=pl.ANY)

    def like(v):
        return pltpu.VMEM(v.shape, v.dtype)

    outs = (weight_grad, input_grad, base, momentum)
    return pl.pallas_call(
        finish_kernel,
        out_shape=[jax.ShapeDtypeStruct(v.shape, v.dtype) for v in outs],
        in_specs=[anywhere] * 5,
        out_specs=[anywhere] * 4,
        scratch_shapes=[like(v) for v in (weight_grad, input_grad, mean_delta, base, momentum, base, momentum)]
        + [pltpu.SemaphoreType.DMA((pieces + 4,)), pltpu.SemaphoreType.DMA((pieces + 3,))],
        compiler_params=pltpu.CompilerParams(vmem_limit_bytes=60 * 2**20),
        name="finish",
    )(weight_grad, input_grad, mean_delta, base, momentum)


def body(
    activations,
    key_target,
    key_weight,
    fragment_base,
    fragment_momentum,
    delta_codes,
    block_scale,
    code_table,
):
    weight_grad, input_grad, mean_delta = inner_step(
        activations, key_target, key_weight, delta_codes, block_scale, code_table
    )
    weight_grad, input_grad, new_base, new_momentum = finish(
        weight_grad, input_grad, mean_delta, fragment_base, fragment_momentum
    )
    return (weight_grad, input_grad, new_base, new_momentum)


def solution(mesh):
    placed = (
        P(("worker", "fsdp"), None),
        P(("worker", "fsdp"), None),
        P(("worker", "fsdp"), None),
        P("fsdp", None),
        P("fsdp", None),
        P(("worker", "fsdp"), None),
        P(("worker", "fsdp"), None),
        P(),
    )
    return jax.shard_map(
        body,
        mesh=mesh,
        in_specs=placed,
        out_specs=(
            P(("worker", "fsdp"), None),
            P(("worker", "fsdp"), None),
            P("fsdp", None),
            P("fsdp", None),
        ),
        check_vma=False,
    )
```

time: 318 us -> 116 us (0.36)
  the two profiles are of different devices: /device:TPU:24 before, /device:TPU:72 now
where the time goes in v2:
time: 116 us
  Pallas kernels  115 us (99%)
    pallas_call x1, Pallas kernels, inner_step(): pl.pallas_call(kernel, out_shape=(jax.ShapeDtypeStruct((rows, kv), F32),...  110 us
    pallas_call x1, Pallas kernels, finish(): pl.pallas_call(finish_kernel, out_shape=[jax.ShapeDtypeStruct(v.shape, v....  5.27 us

profile of v2, /device:TPU:72, one launch (start us, length us, event | category | flops | bytes accessed | tf_op | source)
XLA Modules:
  0.0 115.9 jit_solution(3865420766820702595)
XLA Ops:
  0.6 109.8 %inner_step.1 = (f32[144,1024]{1,0:T(8,128)}, bf16[512,4608]{1,0:T(8,128)(2,1)}, f32[16,4608]{1,0:T(8,128)}) custom-call(f32[16]{0:T(128)} %table.1, bf16[512,4608]{1,0:T(8,128)(2,1)} %a_hbm.1, bf16[512,1024]{1,0:T(8,128)(2,1)} %t_hbm.1, bf16[144,1024]{1,0:T(8,128)(2,1)} %w_hbm.1, s32[16,4608]{1,0:T(8,128)} %code_hbm.1, f32[16,36]{1,0:T(8,128)} %scale_hbm.1), custom_call_target="tpu_custom_call" | custom-call | flops 14495514624 | bytes 67108864 | tf_op jit(solution)/shard_map/inner_step/pallas_call | solution.py:461
  110.4 5.3 %finish.1 = (f32[144,1024]{1,0:T(8,128)}, bf16[512,4608]{1,0:T(8,128)(2,1)}, f32[16,4608]{1,0:T(8,128)}, f32[16,4608]{1,0:T(8,128)}) custom-call(f32[144,1024]{1,0:T(8,128)} %get-tuple-element.7.wg_in, bf16[512,4608]{1,0:T(8,128)(2,1)} %get-tuple-element.8.ig_in, f32[16,4608]{1,0:T(8,128)} %get-tuple-element.9.mean_in, f32[16,4608]{1,0:T(8,128)} %base_in.1, ...), custom_call_target="tpu_custom_call" | custom-call | tf_op jit(solution)/shard_map/finish/pallas_call | solution.py:559

commit v3 on v2

--- a/solution.py
+++ b/solution.py
@@ -8,8 +8,9 @@
 BLOCK = 128
 NZ, NX, NC = 4, 4, 2
 NY, NH = 4, 2
-WIDTHS = (1, 2, 2, 2, 1)
-MIXED = (0, 1, 1, 1, 0)
+WIDTHS = (2, 2, 2, 2)
+MIXED = (0, 1, 1, 1)
+MIXED_BACK = (1, 1, 1, 0)
 
 MESH = pl.DeviceIdType.MESH
 F32, BF16 = jnp.float32, jnp.bfloat16
@@ -31,8 +32,11 @@
     code, bscale, dl, dyr, dz, mean,
     lsem, csem, wsem, tsem, osem, isem, msem,
     ag_s, ag_r, rs_s, rs_r, dl_s, dl_r,
+    gh_s, gh_r, gp_s, gp_r, rh_s, rh_r, rp_s, rp_r,
 ):
     parts = len(w)
+    mix = [sum(MIXED[:s]) for s in range(parts)]
+    mix_r = [sum(MIXED_BACK[:s]) for s in range(parts)]
     tokens, d = a.shape
     rows = w[0].shape[3]
     width = [p.shape[4] for p in w]
@@ -40,6 +44,8 @@
     half = rows // 9
     low = [rows - 2 * half * m for m in MIXED]
     lows = [pl.ds(0, n) for n in low]
+    low_r = [rows - 2 * half * m for m in MIXED_BACK]
+    lows_r = [pl.ds(0, n) for n in low_r]
     first = rows - 2 * half
     hi, hi0, hi1 = pl.ds(first, 2 * half), pl.ds(first, half), pl.ds(first + half, half)
     scale = 1.0 / (tokens * NZ * NX * NC) ** 0.5
@@ -94,7 +100,7 @@
 
     sent = []
 
-    def send(src, dst, ss, rs, to, cond=None):
+    def send(src, dst, ss, rs, to, cond=None, group=False):
         cp = pltpu.make_async_remote_copy(
             src_ref=src, dst_ref=dst, send_sem=ss, recv_sem=rs, device_id=to, device_id_type=MESH
         )
@@ -102,7 +108,8 @@
             cp.start()
         else:
             pl.when(cond)(cp.start)
-        sent.append((cp, cond))
+        if not group:
+            sent.append((cp, cond))
 
     def arrive(dst, rs):
         pltpu.make_async_remote_copy(
@@ -121,13 +128,13 @@
 
     there = guard(lambda s: 0 <= s < parts)
     if_mixed = guard(lambda s: 0 <= s < parts and MIXED[s])
+    if_mixed_r = guard(lambda s: 0 <= s < parts and MIXED_BACK[s])
 
     @there
     def z_send(s):
-        w_in(s).wait()
         for k in (3, 2, 1):
             blk = w[s].at[z, x, c, lows[s]]
-            send(blk, blk, ag_s.at[s, k - 1], ag_r.at[s, k - 1], dev(zup[k], x, c))
+            send(blk, blk, ag_s.at[s, 0], ag_r.at[s, k - 1], dev(zup[k], x, c), group=True)
 
     @there
     def z_wait(s):
@@ -137,17 +144,17 @@
     @there
     def x1_send(s):
         line = w[s].at[:, x, c, lows[s]]
-        send(line, line, ag_s.at[s, 3], ag_r.at[s, 3], DP)
-        send(line, line, ag_s.at[s, 4], ag_r.at[s, 4], DM)
+        send(line, line, ag_s.at[s, 1], ag_r.at[s, 3], DP, group=True)
+        send(line, line, ag_s.at[s, 1], ag_r.at[s, 4], DM, group=True)
 
     @there
     def x2_send(s):
         arrive(w[s].at[:, xm, c, lows[s]], ag_r.at[s, 3])
         up = w[s].at[pl.ds(0, 2), xm, c, lows[s]]
-        send(up, up, ag_s.at[s, 5], ag_r.at[s, 5], DP)
+        send(up, up, ag_s.at[s, 2], ag_r.at[s, 5], DP, group=True)
         arrive(w[s].at[:, xp, c, lows[s]], ag_r.at[s, 4])
         down = w[s].at[pl.ds(2, 2), xp, c, lows[s]]
-        send(down, down, ag_s.at[s, 6], ag_r.at[s, 6], DM)
+        send(down, down, ag_s.at[s, 2], ag_r.at[s, 6], DM, group=True)
 
     @there
     def x2_wait(s):
@@ -157,50 +164,50 @@
     @there
     def d_send(s, k):
         line = w[s].at[:, lines[k], c, lows[s]]
-        send(line, line, ag_s.at[s, 7 + k], ag_r.at[s, 7 + k], DS)
+        send(line, line, ag_s.at[s, 3], ag_r.at[s, 7 + k], DS, group=True)
 
     @if_mixed
     def d_send_hi(s):
         rest = w[s].at[:, :, c, hi]
-        send(rest, rest, ag_s.at[s, 11], ag_r.at[s, 11], DS)
+        send(rest, rest, gh_s.at[mix[s], 0], gh_r.at[mix[s], 0], DS)
 
     @there
     def d_wait(s):
         for k in range(4):
             arrive(w[s].at[:, lines[k], co, lows[s]], ag_r.at[s, 7 + k])
         if MIXED[s]:
-            arrive(w[s].at[:, :, co, hi], ag_r.at[s, 11])
+            arrive(w[s].at[:, :, co, hi], gh_r.at[mix[s], 0])
 
     @if_mixed
     def h1_send(s):
         blk = w[s].at[z, x, c, hi]
-        send(blk, blk, ag_s.at[s, 12], ag_r.at[s, 12], DP)
-        send(blk, blk, ag_s.at[s, 13], ag_r.at[s, 13], DM)
+        send(blk, blk, gh_s.at[mix[s], 1], gh_r.at[mix[s], 1], DP, group=True)
+        send(blk, blk, gh_s.at[mix[s], 1], gh_r.at[mix[s], 2], DM, group=True)
 
     @if_mixed
     def h2_send(s):
-        arrive(w[s].at[z, xm, c, hi], ag_r.at[s, 12])
+        arrive(w[s].at[z, xm, c, hi], gh_r.at[mix[s], 1])
         up = w[s].at[z, xm, c, hi0]
-        send(up, up, ag_s.at[s, 14], ag_r.at[s, 14], DP)
-        arrive(w[s].at[z, xp, c, hi], ag_r.at[s, 13])
+        send(up, up, gh_s.at[mix[s], 2], gh_r.at[mix[s], 3], DP, group=True)
+        arrive(w[s].at[z, xp, c, hi], gh_r.at[mix[s], 2])
         down = w[s].at[z, xp, c, hi1]
-        send(down, down, ag_s.at[s, 15], ag_r.at[s, 15], DM)
+        send(down, down, gh_s.at[mix[s], 2], gh_r.at[mix[s], 4], DM, group=True)
 
     @if_mixed
     def h2_wait(s):
-        arrive(w[s].at[z, xo, c, hi0], ag_r.at[s, 14])
-        arrive(w[s].at[z, xo, c, hi1], ag_r.at[s, 15])
+        arrive(w[s].at[z, xo, c, hi0], gh_r.at[mix[s], 3])
+        arrive(w[s].at[z, xo, c, hi1], gh_r.at[mix[s], 4])
 
     @if_mixed
     def hop_send(s, k):
         up, dn = w[s].at[zdn[k - 1], :, c, hi], w[s].at[zup[k - 1], :, c, hi]
-        send(up, up, ag_s.at[s, 15 + k], ag_r.at[s, 15 + k], DU, (z >= k - 1) & (z < NZ - 1))
-        send(dn, dn, ag_s.at[s, 18 + k], ag_r.at[s, 18 + k], DD, (z + k <= NZ) & (z > 0))
+        send(up, up, gp_s.at[mix[s], k - 1], gp_r.at[mix[s], k - 1], DU, (z >= k - 1) & (z < NZ - 1))
+        send(dn, dn, gp_s.at[mix[s], k + 2], gp_r.at[mix[s], k + 2], DD, (z + k <= NZ) & (z > 0))
 
     @if_mixed
     def hop_wait(s, k):
-        pl.when(z >= k)(lambda: arrive(w[s].at[zdn[k], :, c, hi], ag_r.at[s, 15 + k]))
-        pl.when(z + k < NZ)(lambda: arrive(w[s].at[zup[k], :, c, hi], ag_r.at[s, 18 + k]))
+        pl.when(z >= k)(lambda: arrive(w[s].at[zdn[k], :, c, hi], gp_r.at[mix[s], k - 1]))
+        pl.when(z + k < NZ)(lambda: arrive(w[s].at[zup[k], :, c, hi], gp_r.at[mix[s], k + 2]))
 
     def transpose():
         a_in.wait()
@@ -218,7 +225,7 @@
         xt = lines[k]
         q = jnp.dot(at[:, xt].reshape(slab, tokens), e[s][...], preferred_element_type=F32)
         g[s][:, xt] = q.astype(BF16).reshape(NZ, NC, rows, width[s])
-        send(g[s].at[:, xt, co], dr[s].at[:, xt], rs_s.at[s, k], rs_r.at[s, k], DS)
+        send(g[s].at[:, xt, co], dr[s].at[:, xt], rs_s.at[s, 0], rs_r.at[s, k], DS, group=True)
 
     def back(j):
         er = jnp.concatenate([e[s][...] for s in range(parts)], axis=1)
@@ -245,11 +252,11 @@
     @there
     def r1(s):
         merge(s, 0)
-        send(g[s].at[pl.ds(0, 2), xo, c, lows[s]], x2r[s].at[0], rs_s.at[s, 4], rs_r.at[s, 4], DP)
-        send(g[s].at[pl.ds(2, 2), xo, c, lows[s]], x2r[s].at[1], rs_s.at[s, 5], rs_r.at[s, 5], DM)
+        send(g[s].at[pl.ds(0, 2), xo, c, lows_r[s]], x2r[s].at[0], rs_s.at[s, 1], rs_r.at[s, 4], DP, group=True)
+        send(g[s].at[pl.ds(2, 2), xo, c, lows_r[s]], x2r[s].at[1], rs_s.at[s, 1], rs_r.at[s, 5], DM, group=True)
         for k in (1, 2, 3):
             merge(s, k)
-        if MIXED[s]:
+        if MIXED_BACK[s]:
             hop(s, 1)
 
     def hop(s, k):
@@ -259,26 +266,26 @@
 
             @pl.when(goes_up & (z > 0))
             def _():
-                arrive(zc[s].at[0, k - 2], rs_r.at[s, 9 + k])
+                arrive(zc[s].at[0, k - 2], rp_r.at[mix_r[s], k - 2])
                 g[s][up, :, c, first:] = plus(g[s][up, :, c, first:], zc[s][0, k - 2]).astype(BF16)
 
             @pl.when(goes_dn & (z < NZ - 1))
             def _():
-                arrive(zc[s].at[1, k - 2], rs_r.at[s, 12 + k])
+                arrive(zc[s].at[1, k - 2], rp_r.at[mix_r[s], k + 1])
                 g[s][dn, :, c, first:] = plus(g[s][dn, :, c, first:], zc[s][1, k - 2]).astype(BF16)
 
-        send(g[s].at[up, :, c, hi], zc[s].at[0, k - 1], rs_s.at[s, 10 + k], rs_r.at[s, 10 + k], DU, goes_up)
-        send(g[s].at[dn, :, c, hi], zc[s].at[1, k - 1], rs_s.at[s, 13 + k], rs_r.at[s, 13 + k], DD, goes_dn)
+        send(g[s].at[up, :, c, hi], zc[s].at[0, k - 1], rp_s.at[mix_r[s], k - 1], rp_r.at[mix_r[s], k - 1], DU, goes_up)
+        send(g[s].at[dn, :, c, hi], zc[s].at[1, k - 1], rp_s.at[mix_r[s], k + 2], rp_r.at[mix_r[s], k + 2], DD, goes_dn)
 
     @there
     def r2(s):
         arrive(x2r[s].at[0], rs_r.at[s, 4])
-        g[s][0:2, xp, c, :low[s]] = plus(g[s][0:2, xp, c, :low[s]], x2r[s][0]).astype(BF16)
-        send(g[s].at[:, xp, c, lows[s]], x1r[s].at[0], rs_s.at[s, 6], rs_r.at[s, 6], DP)
+        g[s][0:2, xp, c, :low_r[s]] = plus(g[s][0:2, xp, c, :low_r[s]], x2r[s][0]).astype(BF16)
+        send(g[s].at[:, xp, c, lows_r[s]], x1r[s].at[0], rs_s.at[s, 2], rs_r.at[s, 6], DP, group=True)
         arrive(x2r[s].at[1], rs_r.at[s, 5])
-        g[s][2:4, xm, c, :low[s]] = plus(g[s][2:4, xm, c, :low[s]], x2r[s][1]).astype(BF16)
-        send(g[s].at[:, xm, c, lows[s]], x1r[s].at[1], rs_s.at[s, 7], rs_r.at[s, 7], DM)
-        if MIXED[s]:
+        g[s][2:4, xm, c, :low_r[s]] = plus(g[s][2:4, xm, c, :low_r[s]], x2r[s][1]).astype(BF16)
+        send(g[s].at[:, xm, c, lows_r[s]], x1r[s].at[1], rs_s.at[s, 2], rs_r.at[s, 7], DM, group=True)
+        if MIXED_BACK[s]:
             hop(s, 2)
 
     @there
@@ -287,51 +294,51 @@
         arrive(x1r[s].at[1], rs_r.at[s, 7])
 
         def x_sum(j):
-            return plus(g[s][j, x, c, :low[s]], x1r[s][0, j]) + x1r[s][1, j].astype(F32)
+            return plus(g[s][j, x, c, :low_r[s]], x1r[s][0, j]) + x1r[s][1, j].astype(F32)
 
         for k in (3, 2, 1):
             j = zup[k]
-            g[s][j, x, c, :low[s]] = x_sum(j).astype(BF16)
-            send(g[s].at[j, x, c, lows[s]], zr[s].at[k - 1], rs_s.at[s, 7 + k], rs_r.at[s, 7 + k], dev(j, x, c))
-        wg[: low[s], start[s] : start[s] + width[s]] = x_sum(z)
-        if MIXED[s]:
+            g[s][j, x, c, :low_r[s]] = x_sum(j).astype(BF16)
+            send(g[s].at[j, x, c, lows_r[s]], zr[s].at[k - 1], rs_s.at[s, 3], rs_r.at[s, 7 + k], dev(j, x, c), group=True)
+        wg[: low_r[s], start[s] : start[s] + width[s]] = x_sum(z)
+        if MIXED_BACK[s]:
             hop(s, 3)
 
-    @if_mixed
+    @if_mixed_r
     def r4(s):
         @pl.when(z > 0)
         def _():
-            arrive(zc[s].at[0, 2], rs_r.at[s, 13])
+            arrive(zc[s].at[0, 2], rp_r.at[mix_r[s], 2])
             g[s][z, :, c, first:] = plus(g[s][z, :, c, first:], zc[s][0, 2]).astype(BF16)
 
         @pl.when(z < NZ - 1)
         def _():
-            arrive(zc[s].at[1, 2], rs_r.at[s, 16])
+            arrive(zc[s].at[1, 2], rp_r.at[mix_r[s], 5])
             g[s][z, :, c, first:] = plus(g[s][z, :, c, first:], zc[s][1, 2]).astype(BF16)
 
-        send(g[s].at[z, xo, c, hi0], hx2[s].at[0], rs_s.at[s, 17], rs_r.at[s, 17], DP)
-        send(g[s].at[z, xo, c, hi1], hx2[s].at[1], rs_s.at[s, 18], rs_r.at[s, 18], DM)
-
-    @if_mixed
+        send(g[s].at[z, xo, c, hi0], hx2[s].at[0], rh_s.at[mix_r[s], 0], rh_r.at[mix_r[s], 0], DP, group=True)
+        send(g[s].at[z, xo, c, hi1], hx2[s].at[1], rh_s.at[mix_r[s], 0], rh_r.at[mix_r[s], 1], DM, group=True)
+
+    @if_mixed_r
     def r5(s):
-        arrive(hx2[s].at[0], rs_r.at[s, 17])
+        arrive(hx2[s].at[0], rh_r.at[mix_r[s], 0])
         g[s][z, xp, c, first : first + half] = plus(g[s][z, xp, c, first : first + half], hx2[s][0]).astype(BF16)
-        send(g[s].at[z, xp, c, hi], hx1[s].at[0], rs_s.at[s, 19], rs_r.at[s, 19], DP)
-        arrive(hx2[s].at[1], rs_r.at[s, 18])
+        send(g[s].at[z, xp, c, hi], hx1[s].at[0], rh_s.at[mix_r[s], 1], rh_r.at[mix_r[s], 2], DP, group=True)
+        arrive(hx2[s].at[1], rh_r.at[mix_r[s], 1])
         g[s][z, xm, c, first + half :] = plus(g[s][z, xm, c, first + half :], hx2[s][1]).astype(BF16)
-        send(g[s].at[z, xm, c, hi], hx1[s].at[1], rs_s.at[s, 20], rs_r.at[s, 20], DM)
+        send(g[s].at[z, xm, c, hi], hx1[s].at[1], rh_s.at[mix_r[s], 1], rh_r.at[mix_r[s], 3], DM, group=True)
 
     @there
     def r6(s):
         here = slice(start[s], start[s] + width[s])
-        total = wg[: low[s], here]
+        total = wg[: low_r[s], here]
         for k in (1, 2, 3):
             arrive(zr[s].at[k - 1], rs_r.at[s, 7 + k])
             total = total + zr[s][k - 1].astype(F32)
-        wg[: low[s], here] = total * scale
-        if MIXED[s]:
-            arrive(hx1[s].at[0], rs_r.at[s, 19])
-            arrive(hx1[s].at[1], rs_r.at[s, 20])
+        wg[: low_r[s], here] = total * scale
+        if MIXED_BACK[s]:
+            arrive(hx1[s].at[0], rh_r.at[mix_r[s], 2])
+            arrive(hx1[s].at[1], rh_r.at[mix_r[s], 3])
             rest = plus(g[s][z, x, c, first:], hx1[s][0]) + hx1[s][1].astype(F32)
             wg[first:, here] = rest * scale
         wg_out(s).start()
@@ -374,49 +381,53 @@
         for q in range(NY):
             mean_out(q).start()
 
+    w_in(0).wait()
     z_send(0)
+    for s in range(parts):
+        if s > 0:
+            w_in(s).wait()
+        h1_send(s)
     z_send(1)
-    h1_send(1)
     delta_send()
     z_wait(0)
     x1_send(0)
     d_send(0, 3)
-    h2_send(1)
+    for s in range(parts):
+        h2_send(s)
     z_send(2)
-    h1_send(2)
     transpose()
-    delta_pair()
     z_wait(1)
     x1_send(1)
     d_send(1, 3)
+    for s in range(parts):
+        h2_wait(s)
+        hop_send(s, 1)
+    delta_pair()
     for i in range(parts + 1):
-        h2_wait(i + 1)
-        hop_send(i + 1, 1)
-        hop_wait(i, 2)
-        hop_send(i, 3)
         x2_send(i)
         d_send(i, 1)
         d_send(i, 2)
         z_send(i + 3)
-        h1_send(i + 3)
-        h2_send(i + 2)
         z_wait(i + 2)
         x1_send(i + 2)
         d_send(i + 2, 3)
+        r3(i - 4)
+        r2(i - 3)
         r1(i - 2)
-        r2(i - 3)
-        r3(i - 4)
         d_wait(i - 1)
         project(i - 1)
+        if i < 2:
+            for s in range(parts):
+                hop_wait(s, 1 + i)
+                hop_send(s, 2 + i)
         x2_wait(i)
         d_send(i, 0)
-        hop_wait(i + 1, 1)
-        hop_send(i + 1, 2)
         for k in range(4):
             grad_rows(i - 1, k)
-        hop_wait(i, 3)
-        d_send_hi(i)
         if i == 1:
+            for s in range(parts):
+                hop_wait(s, 3)
+                d_send_hi(s)
             delta_share()
         if i == 2:
             delta_out()
@@ -430,6 +441,25 @@
         back(i - parts - 1)
     r6(parts - 1)
 
+    def all_sent(total, sem):
+        pltpu.make_async_remote_copy(
+            src_ref=total, dst_ref=total, send_sem=sem, recv_sem=sem, device_id=DS, device_id_type=MESH
+        ).wait_send()
+
+    for s in range(parts):
+        lo = lows[s]
+        all_sent(w[s].at[pl.ds(0, 3), x, c, lo], ag_s.at[s, 0])
+        all_sent(w[s].at[:, pl.ds(0, 2), c, lo], ag_s.at[s, 1])
+        all_sent(w[s].at[:, x, c, lo], ag_s.at[s, 2])
+        all_sent(w[s].at[:, :, c, lo], ag_s.at[s, 3])
+        for n, total in enumerate((dr, x2r, x1r, zr)):
+            all_sent(total[s], rs_s.at[s, n])
+        if MIXED[s]:
+            all_sent(w[s].at[z, pl.ds(0, 2), c, hi], gh_s.at[mix[s], 1])
+            all_sent(w[s].at[z, x, c, hi], gh_s.at[mix[s], 2])
+        if MIXED_BACK[s]:
+            all_sent(hx2[s], rh_s.at[mix_r[s], 0])
+            all_sent(hx1[s], rh_s.at[mix_r[s], 1])
     for cp, cond in sent:
         if cond is None:
             cp.wait_send()
@@ -449,9 +479,10 @@
     frag = delta_codes.shape[0]
     widths = [kv * n // sum(WIDTHS) for n in WIDTHS]
     parts = len(widths)
+    mixed, mixed_r = max(1, sum(MIXED)), max(1, sum(MIXED_BACK))
     half = rows // 9
     nhi = 2 * half
-    low = [rows - nhi * m for m in MIXED]
+    low = [rows - nhi * m for m in MIXED_BACK]
     dma = pltpu.SemaphoreType.DMA
 
     def each(*shape):
@@ -496,12 +527,20 @@
             dma((parts,)),
             dma((NZ,)),
             dma((NY,)),
-            dma((parts, 22)),
-            dma((parts, 22)),
-            dma((parts, 21)),
-            dma((parts, 21)),
+            dma((parts, 4)),
+            dma((parts, 11)),
+            dma((parts, 4)),
+            dma((parts, 11)),
             dma((7,)),
             dma((7,)),
+            dma((mixed, 3)),
+            dma((mixed, 5)),
+            dma((mixed, 6)),
+            dma((mixed, 6)),
+            dma((mixed_r, 2)),
+            dma((mixed_r, 4)),
+            dma((mixed_r, 6)),
+            dma((mixed_r, 6)),
         ],
         compiler_params=pltpu.CompilerParams(
             collective_id=0, has_side_effects=True, vmem_limit_bytes=60 * 2**20

time: 116 us -> 114 us (0.983)
  the two profiles are of different devices: /device:TPU:72 before, /device:TPU:24 now
where the time goes in v3:
time: 114 us
  Pallas kernels  113 us (99%)
    pallas_call x1, Pallas kernels, inner_step(): pl.pallas_call(kernel, out_shape=(jax.ShapeDtypeStruct((rows, kv), F32),...  108 us
    pallas_call x1, Pallas kernels, finish(): pl.pallas_call(finish_kernel, out_shape=[jax.ShapeDtypeStruct(v.shape, v....  5.27 us

profile of v3, /device:TPU:24, one launch (start us, length us, event | category | flops | bytes accessed | tf_op | source)
XLA Modules:
  0.0 114.1 jit_solution(11687064038356167967)
XLA Ops:
  0.6 108.1 %inner_step.1 = (f32[144,1024]{1,0:T(8,128)}, bf16[512,4608]{1,0:T(8,128)(2,1)}, f32[16,4608]{1,0:T(8,128)}) custom-call(f32[16]{0:T(128)} %table.1, bf16[512,4608]{1,0:T(8,128)(2,1)} %a_hbm.1, bf16[512,1024]{1,0:T(8,128)(2,1)} %t_hbm.1, bf16[144,1024]{1,0:T(8,128)(2,1)} %w_hbm.1, s32[16,4608]{1,0:T(8,128)} %code_hbm.1, f32[16,36]{1,0:T(8,128)} %scale_hbm.1), custom_call_target="tpu_custom_call" | custom-call | flops 14495514624 | bytes 67108864 | tf_op jit(solution)/shard_map/inner_step/pallas_call | solution.py:492
  108.7 5.3 %finish.1 = (f32[144,1024]{1,0:T(8,128)}, bf16[512,4608]{1,0:T(8,128)(2,1)}, f32[16,4608]{1,0:T(8,128)}, f32[16,4608]{1,0:T(8,128)}) custom-call(f32[144,1024]{1,0:T(8,128)} %get-tuple-element.7.wg_in, bf16[512,4608]{1,0:T(8,128)(2,1)} %get-tuple-element.8.ig_in, f32[16,4608]{1,0:T(8,128)} %get-tuple-element.9.mean_in, f32[16,4608]{1,0:T(8,128)} %base_in.1, ...), custom_call_target="tpu_custom_call" | custom-call | tf_op jit(solution)/shard_map/finish/pallas_call | solution.py:598
